TPU v7x, 512 devices: a whole 4x4x16 slice. The times are simulated.
512 devices in a mesh: row: 8 (over x, core), col: 64 (over y, z).
Axes of the slice: x: 4, y: 4, z: 16, core: 2. Of those that a mesh axis runs over, the one named last changes fastest.
Arguments:
- diag_factors: bfloat16 [3, 512, 512], replicated, as said below
- panel_v: bfloat16 [64, 2, 512, 128], P('row', None, 'col'), may hold values from -2.515625 to 2.515625
- ranks: int32 [64, 2], P('row'), may hold values from 32 to 128, as said below
Outputs:
- panel_factors: bfloat16 [64, 1024, 256], P('row', 'col')
- update_cores: float32 [64, 64, 256, 256], P('row', 'col')
Inputs may be any that keep to these rules, and one draw needn't show every extreme that they name: `ranks`: every panel tile has rank at least 32; the tiles of array row 0 have rank 128. `diag_factors`: inverse0 and inverse1 are lower triangular with positive diagonals.
All inputs are finite; a program needn't handle non-finite values.
Results may differ from a plain program's by a relative error of at most 0.0046.
Values may be sent and summed in bfloat16 or wider, within the bound.
No kernel may reach another device: no remote copies, remote signals or barrier semaphores. Data moves between devices by JAX's collectives and lax.ppermute only.
A program may use at most 64 MiB of HBM per device.

v0:
```python
import jax
import jax.numpy as jnp
from jax import lax
from jax.sharding import PartitionSpec as P


def from_root(block, axis, source):
    block = jnp.where(lax.axis_index(axis) == source, block, jnp.zeros_like(block))
    return lax.psum(block, axis)


def assemble(w_block, lower, right):
    top = jnp.concatenate([w_block, jnp.zeros_like(w_block)], axis=-1)
    bottom = jnp.concatenate([lower, right], axis=-1)
    return jnp.concatenate([top, bottom], axis=-2)


def shards(diag_factors, panel_v, ranks):
    rows_dev = panel_v.shape[0]
    rank_max = panel_v.shape[3]
    nrow = lax.axis_size("row")
    ncol = lax.axis_size("col")
    prow = lax.axis_index("row")
    qcol = lax.axis_index("col")
    inverse0 = diag_factors[0]
    couple = diag_factors[1]
    inverse1 = diag_factors[2]
    columns = jnp.arange(rank_max, dtype=jnp.int32)
    keep = columns[None, None, :] < ranks[:, :, None]
    masked = jnp.where(keep[:, :, None, :], panel_v, jnp.zeros_like(panel_v))
    whole = lax.all_gather(masked, "col", axis=2, tiled=True)
    w_block = jnp.einsum(
        "nm,tmr->tnr", inverse0, whole[:, 0], preferred_element_type=jnp.float32
    ).astype(jnp.bfloat16)
    right = jnp.einsum(
        "nm,tmr->tnr", inverse1, whole[:, 1], preferred_element_type=jnp.float32
    ).astype(jnp.bfloat16)
    lower = jnp.einsum("nm,tmr->tnr", couple, w_block, preferred_element_type=jnp.float32).astype(
        jnp.bfloat16
    )
    factors = assemble(w_block, lower, right)
    piece = factors.shape[1] // ncol
    factor_share = lax.dynamic_slice_in_dim(factors, qcol * piece, piece, 1)
    owner = qcol % nrow
    local_row = qcol // nrow
    picked = lax.dynamic_index_in_dim(factors, local_row, 0, keepdims=False)
    column_factor = from_root(picked, "row", owner)
    cores = jnp.einsum("tkr,ks->trs", factors, column_factor, preferred_element_type=jnp.float32)
    codes = jnp.arange(rows_dev, dtype=jnp.int32) * nrow + prow
    active = codes > qcol
    cores = jnp.where(active[:, None, None], cores, jnp.zeros_like(cores))
    return (factor_share, cores[:, None])


def solution(mesh):
    placed = (P(), P("row", None, "col", None), P("row", None))
    return jax.shard_map(
        shards,
        mesh=mesh,
        in_specs=placed,
        out_specs=(P("row", "col", None), P("row", "col", None, None)),
        check_vma=False,
    )
```

profile of v0, /device:TPU:8, one launch (start us, length us, event | category | flops | bytes accessed | tf_op | source)
XLA Modules:
  0.0 252.6 jit_solution(16143106622238425557)
XLA Ops:
  7.2 0.0 all-gather.2.cloned.1.call-start
  7.2 0.8 iota_compare_fusion.1
  8.0 1.4 copy_select_fusion
  9.3 0.0 all-gather.2.cloned.1.call-update
  9.4 0.0 all-reduce.3.cloned.1.call-start
  9.4 146.3 %all-gather.2.cloned.1.call-done = bf16[8,2,512,128]{3,0,1,2:T(8,128)(2,1)} async-done(((bf16[8,2,8,128]{3,0,1,2:T(8,128)(2,1)}), bf16[8,2,512,128]{3,0,1,2:T(8,128)(2,1)}) %all-gather.2.cloned.1.call-update) | async-done | bytes 2097168 | tf_op jit(solution)/shard_map/all_gather | solution.py:31
  155.8 1.7 fusion.15
  157.4 0.7 copy.17
  158.1 0.7 copy.18
  158.8 1.8 fusion.2
  160.6 1.8 fusion.4
  162.4 1.8 fusion.3
  164.2 0.0 copy-start.1
  164.2 1.0 copy-done.1
  165.1 0.5 fusion.1
  165.7 0.0 copy-start
  165.7 1.9 copy-done
  167.6 0.8 select_bitcast_fusion.1
  168.4 0.0 all-reduce.3.cloned.1.call-update
  168.5 1.3 constant_dynamic-slice_fusion
  169.7 0.8 copy.13
  170.6 71.2 %all-reduce.3.cloned.1.call-done = bf16[1024,256]{0,1:T(8,128)(2,1)} async-done(((bf16[1024,256]{0,1:T(8,128)(2,1)}), bf16[1024,256]{0,1:T(8,128)(2,1)}) %all-reduce.3.cloned.1.call-update) | async-done | bytes 524304 | tf_op jit(solution)/shard_map/psum | solution.py:9
  241.8 4.0 %select_bitcast_fusion = f32[8,1,256,256]{3,2,1,0:T(8,128)} fusion(pred[8]{0:T(512)(128)(4,1)S(1)} %add_compare_fusion, bf16[1024,256]{0,1:T(8,128)(2,1)} %all-reduce.3.cloned.1.call-done, bf16[8,512,128]{1,2,0:T(8,128)(2,1)S(1)} %fusion.2, bf16[8,512,128]{1,2,0:T(8,128)(2,1)S(1)} %fusion.4, bf16[8,512,128]{1,2,0:T(8,128)(2,1)} %copy-done.1), kind=kOutput, calls=%fused_computation.3 | convolution fusion | flops 1091043328 | bytes 5767176 | tf_op jit(solution)/shard_map/tkr,ks->trs/dot_general | solution.py:48
  (1 shorter events, 0.0 us)
Async XLA Ops:
  7.2 148.6 %all-gather.2.cloned.1.call-start = ((), (), s32[]{:S(2)}) async-start(), calls=%async_computation | async-start | bytes 2129920 | tf_op jit(solution)/shard_map/all_gather | solution.py:31
  9.4 232.4 %all-reduce.3.cloned.1.call-start = ((), (), s32[]{:S(2)}) async-start(), calls=%async_computation.1 | async-start | bytes 1048576 | tf_op jit(solution)/shard_map/psum | solution.py:9
  164.2 1.0 copy-start.1
  165.7 1.9 copy-start
Sparse Core Ops, SparseCore 0:
  11.5 144.1 all-gather.1
  168.6 73.1 all-reduce.2
where the time goes:
time: 253 us
  waiting for transfers between devices  218 us (86%)
  between operations  14.1 us (6%)
  matrix products  9.31 us (4%)
  local copies, waits for them, and re-layouts  8.01 us (3%)
  other arithmetic  3.49 us (1%)
    all_gather x1, waiting for transfers between devices, shards(): whole = lax.all_gather(masked, 'col', axis=2, tiled=True)  146 us
    psum x1, waiting for transfers between devices, from_root(): return lax.psum(block, axis)  71.2 us
    unnamed x7, local copies, waits for them, and re-layouts  5.07 us
  transfers between devices with their start and end apart: 2, of which 2 were waited for; matrix products, arithmetic and copies ran while one was open for 1% of the time, Pallas kernels for 0%

commit v1 on v0

--- a/solution.py
+++ b/solution.py
@@ -28,7 +28,9 @@
     columns = jnp.arange(rank_max, dtype=jnp.int32)
     keep = columns[None, None, :] < ranks[:, :, None]
     masked = jnp.where(keep[:, :, None, :], panel_v, jnp.zeros_like(panel_v))
-    whole = lax.all_gather(masked, "col", axis=2, tiled=True)
+    whole = jnp.concatenate(
+        lax.all_to_all(jnp.stack([masked] * lax.axis_size("col")), "col", 0, 0), axis=2
+    )
     w_block = jnp.einsum(
         "nm,tmr->tnr", inverse0, whole[:, 0], preferred_element_type=jnp.float32
     ).astype(jnp.bfloat16)

time: 253 us -> 216 us (0.85)
  waiting for transfers between devices: 218 us -> 165 us
  starting transfers between devices: 0.08 us -> 18.8 us
  matrix products: 9.31 us -> 6.22 us
    all_gather x1 -> x0, waiting for transfers between devices: 146 us -> none  [shards(): whole = lax.all_gather(masked, 'col', axis=2, tiled=True)]
    all_to_all x0 -> x1, waiting for transfers between devices: none -> 97.4 us  [shards(): lax.all_to_all(jnp.stack([masked] * lax.axis_size('col')), 'col', 0, 0)]
    all_to_all x0 -> x1, starting transfers between devices: none -> 18.7 us  [shards(): lax.all_to_all(jnp.stack([masked] * lax.axis_size('col')), 'col', 0, 0)]
    psum x1, waiting for transfers between devices: 71.2 us -> 67.8 us  [from_root(): return lax.psum(block, axis)]
    unnamed x7 -> x8, local copies, waits for them, and re-layouts: 5.07 us -> 5.33 us
where the time goes in v1:
time: 216 us
  waiting for transfers between devices  165 us (76%)
  starting transfers between devices  18.8 us (9%)
  between operations  14.1 us (7%)
  local copies, waits for them, and re-layouts  8.95 us (4%)
  matrix products  6.22 us (3%)
  other arithmetic  2.21 us (1%)
    all_to_all x1, waiting for transfers between devices, shards(): lax.all_to_all(jnp.stack([masked] * lax.axis_size('col')), 'col', 0, 0)  97.4 us
    psum x1, waiting for transfers between devices, from_root(): return lax.psum(block, axis)  67.8 us
    all_to_all x1, starting transfers between devices, shards(): lax.all_to_all(jnp.stack([masked] * lax.axis_size('col')), 'col', 0, 0)  18.7 us
    unnamed x8, local copies, waits for them, and re-layouts  5.33 us
  transfers between devices with their start and end apart: 2, of which 2 were waited for; matrix products, arithmetic and copies ran while one was open for 1% of the time, Pallas kernels for 0%

profile of v1, /device:TPU:8, one launch (start us, length us, event | category | flops | bytes accessed | tf_op | source)
XLA Modules:
  0.0 215.5 jit_solution(7039342695954034531)
XLA Ops:
  7.2 0.8 copy.16
  7.9 0.1 iota_compare_fusion.1
  8.0 0.8 broadcast_select_fusion
  8.8 1.8 stack.2
  10.6 18.7 %all-to-all-start = ((bf16[64,8,2,8,128]{4,3,2,1,0:T(8,128)(2,1)}), bf16[64,8,2,8,128]{4,3,2,1,0:T(8,128)(2,1)S(1)}, u32[]{:S(2)}, u32[]{:S(2)}) async-start(bf16[64,8,2,8,128]{4,3,2,1,0:T(8,128)(2,1)} %stack.2), calls=%async_computation | async-start | bytes 4194304 | tf_op jit(solution)/shard_map/all_to_all | solution.py:32
  29.3 0.0 all-reduce.3.cloned.1.call-start
  29.4 97.4 %all-to-all-done = bf16[64,8,2,8,128]{4,3,2,1,0:T(8,128)(2,1)S(1)} async-done(((bf16[64,8,2,8,128]{4,3,2,1,0:T(8,128)(2,1)}), bf16[64,8,2,8,128]{4,3,2,1,0:T(8,128)(2,1)S(1)}, u32[]{:S(2)}, u32[]{:S(2)}) %all-to-all-start) | async-done | bytes 2097184 | tf_op jit(solution)/shard_map/all_to_all | solution.py:32
  126.8 0.0 copy-start.2
  126.8 0.5 copy.28
  127.4 0.9 copy-done.2
  128.3 0.8 fusion.2
  129.0 0.8 fusion.4
  129.8 0.7 fusion.3
  130.5 0.0 copy-start.1
  130.5 1.0 copy-done.1
  131.5 0.5 fusion.1
  132.0 0.0 copy-start
  132.0 1.9 copy-done
  134.0 0.8 select_bitcast_fusion.1
  134.8 0.0 all-reduce.3.cloned.1.call-update
  134.8 1.3 constant_dynamic-slice_fusion
  136.1 0.8 copy.21
  136.9 67.8 %all-reduce.3.cloned.1.call-done = bf16[1024,256]{0,1:T(8,128)(2,1)} async-done(((bf16[1024,256]{0,1:T(8,128)(2,1)}), bf16[1024,256]{0,1:T(8,128)(2,1)}) %all-reduce.3.cloned.1.call-update) | async-done | bytes 524304 | tf_op jit(solution)/shard_map/psum | solution.py:9
  204.7 4.0 %select_bitcast_fusion = f32[8,1,256,256]{3,2,1,0:T(8,128)} fusion(pred[8]{0:T(512)(128)(4,1)S(1)} %add_compare_fusion, bf16[1024,256]{0,1:T(8,128)(2,1)} %all-reduce.3.cloned.1.call-done, bf16[8,512,128]{1,2,0:T(8,128)(2,1)S(1)} %fusion.2, bf16[8,512,128]{1,2,0:T(8,128)(2,1)S(1)} %fusion.4, bf16[8,512,128]{1,2,0:T(8,128)(2,1)} %copy-done.1), kind=kOutput, calls=%fused_computation.4 | convolution fusion | flops 1091043328 | bytes 5767176 | tf_op jit(solution)/shard_map/tkr,ks->trs/dot_general | solution.py:50
  (1 shorter events, 0.0 us)
Async XLA Ops:
  10.6 116.2 %all-to-all-start = ((bf16[64,8,2,8,128]{4,3,2,1,0:T(8,128)(2,1)}), bf16[64,8,2,8,128]{4,3,2,1,0:T(8,128)(2,1)S(1)}, u32[]{:S(2)}, u32[]{:S(2)}) async-start(bf16[64,8,2,8,128]{4,3,2,1,0:T(8,128)(2,1)} %stack.2), calls=%async_computation | async-start | bytes 4194304 | tf_op jit(solution)/shard_map/all_to_all | solution.py:32
  29.3 175.4 %all-reduce.3.cloned.1.call-start = ((), (), s32[]{:S(2)}) async-start(), calls=%async_computation.1 | async-start | bytes 1048576 | tf_op jit(solution)/shard_map/psum | solution.py:9
  126.8 1.4 copy-start.2
  130.5 1.0 copy-start.1
  132.0 1.9 copy-start
Sparse Core Ops, SparseCore 0:
  134.9 69.7 all-reduce.2

commit v2 on v0

--- a/solution.py
+++ b/solution.py
@@ -6,7 +6,7 @@
 
 def from_root(block, axis, source):
     block = jnp.where(lax.axis_index(axis) == source, block, jnp.zeros_like(block))
-    return lax.psum(block, axis)
+    return jnp.sum(lax.all_gather(block, axis), axis=0)
 
 
 def assemble(w_block, lower, right):

time: 253 us -> 223 us (0.88)
  the two profiles are of different devices: /device:TPU:8 before, /device:TPU:1 now
where the time goes in v2:
time: 223 us; the launch traced here: 222 us
  waiting for transfers between devices  183 us (82%)
  between operations  14.1 us (6%)
  local copies, waits for them, and re-layouts  9.87 us (4%)
  matrix products  9.09 us (4%)
  other arithmetic  6.41 us (3%)
    all_gather x1, waiting for transfers between devices, shards(): whole = lax.all_gather(masked, 'col', axis=2, tiled=True)  140 us
    all_gather x1, waiting for transfers between devices, from_root(): return jnp.sum(lax.all_gather(block, axis), axis=0)  43.1 us
    unnamed x9, local copies, waits for them, and re-layouts  5.9 us
  transfers between devices with their start and end apart: 2, of which 2 were waited for; matrix products, arithmetic and copies ran while one was open for 1% of the time, Pallas kernels for 0%

profile of v2, /device:TPU:1, one launch (start us, length us, event | category | flops | bytes accessed | tf_op | source)
XLA Modules:
  0.0 222.2 jit_solution(14660856804563983273)
XLA Ops:
  7.2 0.0 all-gather.3.cloned.1.call-start
  7.2 0.8 iota_compare_fusion.1
  8.0 1.4 copy_select_fusion
  9.3 0.0 all-gather.3.cloned.1.call-update
  9.4 0.0 all-gather.5.cloned.1.call-start
  9.4 139.5 %all-gather.3.cloned.1.call-done = bf16[8,2,512,128]{3,0,1,2:T(8,128)(2,1)} async-done(((bf16[8,2,8,128]{3,0,1,2:T(8,128)(2,1)}), bf16[8,2,512,128]{3,0,1,2:T(8,128)(2,1)}) %all-gather.3.cloned.1.call-update) | async-done | bytes 2097168 | tf_op jit(solution)/shard_map/all_gather | solution.py:31
  149.0 1.7 fusion.15
  150.7 0.7 copy.19
  151.4 1.5 copy.20
  152.8 1.8 fusion.2
  154.6 2.1 fusion.4
  156.7 1.8 fusion.3
  158.5 0.0 copy-start.1
  158.5 1.0 copy-done.1
  159.5 0.5 fusion.1
  160.0 0.0 copy-start
  160.0 2.0 copy-done
  162.0 1.0 copy.11
  163.1 0.0 all-gather.5.cloned.1.call-update
  163.1 1.3 constant_dynamic-slice_fusion
  164.4 0.8 copy.14
  165.2 0.0 copy-start.2
  165.2 43.1 %all-gather.5.cloned.1.call-done = bf16[8,1024,256]{2,1,0:T(8,128)(2,1)} async-done(((bf16[1,1024,256]{2,1,0:T(8,128)(2,1)}), bf16[8,1024,256]{2,1,0:T(8,128)(2,1)}) %all-gather.5.cloned.1.call-update) | async-done | bytes 4194320 | tf_op jit(solution)/shard_map/all_gather | solution.py:9
  208.3 3.7 %reduce_sum.12 = bf16[1024,256]{1,0:T(8,128)(2,1)} reduce(bf16[8,1024,256]{2,1,0:T(8,128)(2,1)} %all-gather.5.cloned.1.call-done, bf16[]{:T(256)} %constant.40.clone.1), dimensions={0}, to_apply=%region_0.1 | reduce | flops 1835008 | bytes 4718594 | tf_op jit(solution)/shard_map/reduce_sum | solution.py:9
  212.0 0.0 copy-done.2
  212.0 3.4 %select_bitcast_fusion = f32[8,1,256,256]{3,2,1,0:T(8,128)} fusion(pred[8]{0:T(512)(128)(4,1)S(1)} %add_compare_fusion, bf16[1024,256]{1,0:T(8,128)(2,1)} %reduce_sum.12, bf16[8,512,128]{1,2,0:T(8,128)(2,1)S(1)} %fusion.2, bf16[8,512,128]{1,2,0:T(8,128)(2,1)S(1)} %fusion.4, bf16[8,512,128]{1,2,0:T(8,128)(2,1)S(1)} %copy-done.2), kind=kOutput, calls=%fused_computation.3 | convolution fusion | flops 1091043328 | bytes 5767176 | tf_op jit(solution)/shard_map/tkr,ks->trs/dot_general | solution.py:48
  (2 shorter events, 0.1 us)
Async XLA Ops:
  7.2 141.8 %all-gather.3.cloned.1.call-start = ((), (), s32[]{:S(2)}) async-start(), calls=%async_computation | async-start | bytes 2129920 | tf_op jit(solution)/shard_map/all_gather | solution.py:31
  9.4 198.9 %all-gather.5.cloned.1.call-start = ((), (), s32[]{:S(2)}) async-start(), calls=%async_computation.1 | async-start | bytes 4718592 | tf_op jit(solution)/shard_map/all_gather | solution.py:9
  158.5 1.0 copy-start.1
  160.0 2.0 copy-start
  165.2 46.8 %copy-start.2 = (bf16[8,512,128]{1,2,0:T(8,128)(2,1)S(1)}, bf16[8,512,128]{1,2,0:T(8,128)(2,1)}, u32[]{:S(2)}) copy-start(bf16[8,512,128]{1,2,0:T(8,128)(2,1)} %copy-done.1) | copy-start | bytes 3145732
Sparse Core Ops, SparseCore 0:
  11.5 137.4 all-gather.2
  163.2 45.0 all-gather.4
